TPU v7x, 128 devices: a whole 4x4x4 slice. The times are simulated.
128 devices in a mesh: member: 16 (over y, x_lo, core), tp: 8 (over x_hi, z).
Axes of the slice: x: 4 (x_hi: 2, x_lo: 2; x = x_hi * 2 + x_lo), y: 4, z: 4, core: 2. Of those that a mesh axis runs over, the one named last changes fastest.
Arguments:
- acts: bfloat16 [16, 512, 2560], P('member', None, 'tp'), may hold values from -8 to 8
- weights: bfloat16 [16, 2560, 1024], P('member', 'tp'), may hold values from -6 to 6
Outputs:
- merged: bfloat16 [2560, 1024], P(None, 'tp')
All inputs are finite; a program needn't handle non-finite values.
Results may differ from a plain program's by a relative error of at most 0.005.
Values may be sent and summed in bfloat16 or wider, within the bound.
A program may use at most 256 MiB of HBM per device.

v0:
```python
import jax
import jax.numpy as jnp
from jax import lax
from jax.experimental import pallas as pl
from jax.experimental.pallas import tpu as pltpu
from jax.sharding import PartitionSpec as P

f32, bf16 = jnp.float32, jnp.bfloat16
SHRINK = 0.9
B = 256
H = 128
NT = (((1,), (1,)), ((), ()))
NN = (((1,), (0,)), ((), ()))


def split(x):
    hi = x.astype(bf16)
    return hi, (x - hi.astype(f32)).astype(bf16)


def mm(a, b, dims=NN):
    return lax.dot_general(a, b, dims, preferred_element_type=f32)


def mm3(a, b, dims=NN):
    ah, al = split(a)
    bh, bl = split(b)
    return mm(ah, bh, dims) + (mm(ah, bl, dims) + mm(al, bh, dims))


def tree_sum(terms):
    while len(terms) > 1:
        pairs = [terms[i] + terms[i + 1] for i in range(0, len(terms) - 1, 2)]
        terms = pairs + terms[len(pairs) * 2 :]
    return terms[0]


def inverse_factor(block):
    groups = H // 8
    lane = lax.broadcasted_iota(jnp.int32, (8, H), 1)
    sub = lax.broadcasted_iota(jnp.int32, (8, H), 0)
    a = [block[8 * g : 8 * g + 8, :] for g in range(groups)]
    out = []
    for t in range(groups):
        base = 8 * t
        slab = a[t]
        in_block = (lane >= base) & (lane < base + 8)
        rows = [jnp.broadcast_to(slab[i : i + 1, :], (8, H)) for i in range(8)]
        e = [
            [jnp.broadcast_to(rows[i][:, base + c : base + c + 1], (8, H)) for c in range(i + 1)]
            for i in range(8)
        ]
        r = [jnp.where(in_block, (lane == base + i).astype(f32), rows[i]) for i in range(8)]
        inv = [None] * 8
        piv = [None] * 8
        low = [[None] * 8 for _ in range(8)]
        unit = [[None] * 8 for _ in range(8)]

        def eliminate(c, i):
            r[i] = r[i] - low[i][c] * r[c]
            for j in range(c):
                unit[i][j] = unit[i][j] - low[i][c] * unit[c][j]
            unit[i][c] = -low[i][c]

        for c in range(0, 8, 2):
            d = c + 1
            p, q, s = e[c][c], e[d][c], e[d][d]
            det = p * s - q * q
            inv_p = pl.reciprocal(p, approx=True)
            inv_det = pl.reciprocal(det, approx=True)
            inv[c], inv[d] = inv_p, p * inv_det
            piv[c], piv[d] = p, det * inv_p
            low[d][c] = q * inv_p
            left = {i: e[i][c] * s - e[i][d] * q for i in range(c + 2, 8)}
            right = {i: e[i][d] * p - e[i][c] * q for i in range(c + 2, 8)}
            for i in range(c + 2, 8):
                for j in range(c + 2, i + 1):
                    e[i][j] = e[i][j] - (left[i] * e[j][c] + right[i] * e[j][d]) * inv_det
                low[i][c] = e[i][c] * inv_p
                low[i][d] = right[i] * inv_det
            eliminate(c, d)
            for i in range(c + 2, 8):
                eliminate(c, i)
                eliminate(d, i)
        own = jnp.zeros((8, H), f32)
        for i in range(8):
            own = jnp.where(sub == i, r[i] * lax.rsqrt(piv[i]), own)
        out.append(jnp.where(lane < base + 8, own, 0.0))
        if t + 1 < groups:
            v = [r[i] * inv[i] for i in range(8)]
            z = [tree_sum([v[j]] + [unit[i][j] * v[i] for i in range(j + 1, 8)]) for j in range(8)]
            for g in range(t + 1, groups):
                old = a[g]
                column = [jnp.broadcast_to(old[:, base + j : base + j + 1], (8, H)) for j in range(8)]
                a[g] = jnp.where(in_block, 0.0, old) - tree_sum([column[j] * z[j] for j in range(8)])
    return jnp.concatenate(out, 0)

MESH = pl.DeviceIdType.MESH
TN = (((0,), (0,)), ((), ()))
NS = 7
PARTS = ((0, 3), (3, 2), (5, 2))


def place():
    m = lax.axis_index("member")
    t = lax.axis_index("tp")
    x = (t // 4) * 2 + (m // 2) % 2
    return x, m // 4, t % 4, m % 2


def device(x, y, z, c):
    return ((y * 2 + x % 2) * 2 + c, (x // 2) * 4 + z)


def greet(peers):
    barrier = pltpu.get_barrier_semaphore()
    for peer in peers:
        pl.semaphore_signal(barrier, inc=1, device_id=peer, device_id_type=MESH)
    pl.semaphore_wait(barrier, len(peers))


def remote(src, dst, send, recv, peer):
    return pltpu.make_async_remote_copy(
        src_ref=src, dst_ref=dst, send_sem=send, recv_sem=recv, device_id=peer, device_id_type=MESH
    )


def gather_kernel(a_ref, w_ref, at_ref, wc_ref, wx, send, recv, own):
    x, y, z, c = place()
    xh = x // 2
    t = xh * 4 + z
    other = (1 - xh) * 4 + z
    half = a_ref.shape[0] // 2
    partner = device((x + 2) % 4, y, z, c)
    ring = [device(x, y, (z + d) % 4, c) for d in range(4)]
    greet([partner] + ring[1:])

    def copy(i, src, dst, peer):
        made = remote(src, dst, send.at[i], recv.at[i], peer)
        made.start()
        return made

    def cols(first):
        return pl.ds(pl.multiple_of(first * 128, 128), 128)

    copies = {}
    copies[0] = copy(0, a_ref, at_ref.at[t], partner)
    copies[1] = copy(1, a_ref, at_ref.at[t], ring[1])
    copies[2] = copy(2, a_ref, at_ref.at[t], ring[3])
    far = pl.ds(pl.multiple_of((1 - xh) * 512, 512), 512)
    copies[9] = copy(9, w_ref.at[:, far], wx, partner)
    for d in range(1, 4):
        src = w_ref.at[:, cols(xh * 4 + (z + d) % 4)]
        copies[9 + d] = copy(9 + d, src, wc_ref.at[t], ring[d])
    keep_a = pltpu.make_async_copy(a_ref, at_ref.at[t], own.at[0])
    keep_a.start()
    keep_w = pltpu.make_async_copy(w_ref.at[:, cols(t)], wc_ref.at[t], own.at[1])
    keep_w.start()
    copies[0].wait_recv()
    copies[3] = copy(3, at_ref.at[other], at_ref.at[other], ring[1])
    copies[4] = copy(4, at_ref.at[other], at_ref.at[other], ring[3])
    for at, side in ((0, xh), (2, 1 - xh)):
        before = side * 4 + (z + 3) % 4
        after = side * 4 + (z + 1) % 4
        copies[1 + at].wait_recv()
        part = at_ref.at[before, pl.ds(0, half)]
        copies[5 + at] = copy(5 + at, part, part, ring[1])
        copies[2 + at].wait_recv()
        part = at_ref.at[after, pl.ds(half, half)]
        copies[6 + at] = copy(6 + at, part, part, ring[3])
    copies[9].wait_recv()
    keep_x = pltpu.make_async_copy(wx.at[:, cols(z)], wc_ref.at[other], own.at[2])
    keep_x.start()
    for d in range(1, 4):
        src = wx.at[:, cols((z + d) % 4)]
        copies[12 + d] = copy(12 + d, src, wc_ref.at[other], ring[d])
    for i in (5, 6, 7, 8, 10, 11, 12, 13, 14, 15):
        copies[i].wait_recv()
    for i in range(16):
        copies[i].wait_send()
    keep_a.wait()
    keep_w.wait()
    keep_x.wait()


def gather_acts(acts_t, weight):
    width, rows = acts_t.shape
    vmem = pl.BlockSpec(memory_space=pltpu.VMEM)
    return pl.pallas_call(
        gather_kernel,
        out_shape=(
            jax.ShapeDtypeStruct((8, width, rows), bf16),
            jax.ShapeDtypeStruct((8, width, 128), bf16),
        ),
        in_specs=[vmem, vmem],
        out_specs=(vmem, vmem),
        scratch_shapes=[
            pltpu.VMEM((width, 512), bf16),
            pltpu.SemaphoreType.DMA((16,)),
            pltpu.SemaphoreType.DMA((16,)),
            pltpu.SemaphoreType.DMA((3,)),
        ],
        compiler_params=pltpu.CompilerParams(
            collective_id=0, has_side_effects=True, vmem_limit_bytes=32 * 1024 * 1024
        ),
    )(acts_t, weight)


def product_kernel(at_ref, wc_ref, part_ref, right_ref):
    t = lax.axis_index("tp")
    projected = mm(at_ref[...], wc_ref[...], TN).astype(bf16)
    for i in range(10):
        rows = pl.ds(i * 256, 256)
        own = at_ref[rows, :]
        wide = own.astype(f32)
        diag = jnp.sum(wide * wide, axis=1, keepdims=True)
        scaled = diag * wc_ref[rows, :].astype(f32)
        right_ref[rows, :] = SHRINK * mm(own, projected) + (1.0 - SHRINK) * scaled
    for s in range(NS):
        b = jnp.minimum(s * 8 + t, 54)
        k = 0
        for j in range(1, 10):
            k = k + (b >= 10 * j - j * (j - 1) // 2).astype(jnp.int32)
        i = b - (10 * k - k * (k - 1) // 2) + k
        left = at_ref[pl.ds(pl.multiple_of(i * 256, 256), 256), :]
        right = at_ref[pl.ds(pl.multiple_of(k * 256, 256), 256), :]
        part_ref[s] = mm(left, right, NT)


def products(at, wc):
    vmem = pl.BlockSpec(memory_space=pltpu.VMEM)
    return pl.pallas_call(
        product_kernel,
        out_shape=(
            jax.ShapeDtypeStruct((NS, 256, 256), f32),
            jax.ShapeDtypeStruct((2560, 128), f32),
        ),
        in_specs=[vmem, vmem],
        out_specs=(vmem, vmem),
        compiler_params=pltpu.CompilerParams(vmem_limit_bytes=40 * 1024 * 1024),
    )(at, wc)


def sum_spread_kernel(
    g_ref, r_ref, go_ref, ro_ref, g_pair, r_pair, g_in, r_in, g_own, r_own,
    send, recv, gsend, grecv, rsend, rrecv, own,
):
    x, y, z, c = place()
    coord = (x, y, z)
    q = (x % 2) * 4 + y
    pair = device(x, y, z, 1 - c)
    peers = []
    for d in range(1, 8):
        p = (q + d) % 8
        peers.append((p, device((x // 2) * 2 + p // 4, p % 4, z, c)))

    def along(axis, shift):
        moved = list(coord)
        moved[axis] = (moved[axis] + shift) % 4
        return device(*moved, c)

    ring = [[along(axis, shift) for shift in range(4)] for axis in range(3)]
    near = [ring[axis][shift] for axis in range(3) for shift in (1, 2, 3)]
    greet([pair] + [peer for _, peer in peers] + near)

    first = [
        remote(g_ref.at[:, 1 - c], g_pair, send.at[0], recv.at[0], pair),
        remote(r_ref.at[1 - c], r_pair, send.at[1], recv.at[1], pair),
    ]
    for copy in first:
        copy.start()
    for copy in first:
        copy.wait_recv()
    g_pair[...] = g_pair[...] + g_ref[:, c]
    r_pair[...] = r_pair[...] + r_ref[c]
    second = []
    for d, (p, peer) in enumerate(peers):
        second.append(remote(g_pair.at[:, p], g_in.at[d], send.at[2 + d], recv.at[2 + d], peer))
        second.append(remote(r_pair.at[p], r_in.at[d], send.at[9 + d], recv.at[9 + d], peer))
    for copy in second:
        copy.start()
    for copy in second:
        copy.wait_recv()
    g_sum = g_pair[:, q]
    r_sum = r_pair[q]
    for d in range(7):
        g_sum = g_sum + g_in[d]
        r_sum = r_sum + r_in[d]
    g_own[...] = g_sum
    r_own[...] = r_sum
    started = first + second

    keep_g = pltpu.make_async_copy(g_own, go_ref.at[:, c, x, y, z], own.at[0])
    keep_r = pltpu.make_async_copy(r_own, ro_ref.at[c * 8 + q], own.at[1])
    keep_g.start()
    keep_r.start()

    def view(p, phase, value, rows=None):
        order = (p, (p + 1) % 3, (p + 2) % 3)
        index = list(coord)
        for axis in order[:phase]:
            index[axis] = pl.ds(0, 4)
        index[order[phase]] = value
        start, count = PARTS[p]
        index = [pl.ds(start, count), c] + index
        if rows is not None:
            index.append(pl.ds(rows, 8))
        return go_ref.at[tuple(index)]

    def copy(ref, sems, i, peer, src=None):
        made = remote(ref if src is None else src, ref, sems[0].at[i], sems[1].at[i], peer)
        made.start()
        started.append(made)
        return made

    g_sems, r_sems = (gsend, grecv), (rsend, rrecv)
    for phase in range(2):
        waits = []
        for p in range(3):
            axis = (p + phase) % 3
            mine = view(p, phase, coord[axis])
            base = (p * 3 + phase) * 4
            source = g_own.at[pl.ds(*PARTS[p])] if phase == 0 else None
            for n, shift in enumerate((2, 1, 3)):
                waits.append(copy(mine, g_sems, base + n, ring[axis][shift], source))
        if phase == 0:
            r_copies = [
                copy(ro_ref.at[c * 8 + q], r_sems, d, peer, r_own)
                for d, (_, peer) in enumerate(peers)
            ]
            keep_g.wait()
            keep_r.wait()
        for made in waits:
            made.wait_recv()
    last = []
    hops = []
    for p in range(3):
        axis = (p + 2) % 3
        mine = view(p, 2, coord[axis])
        base = (p * 3 + 2) * 4
        hops.append((copy(mine, g_sems, base, ring[axis][1]), copy(mine, g_sems, base + 1, ring[axis][3])))
        last.append(copy(mine, g_sems, 36 + p * 4, pair))
    for made in r_copies:
        made.wait_recv()
    last.append(copy(ro_ref.at[pl.ds(pl.multiple_of(c * 8, 8), 8)], r_sems, 7, pair))
    forwards = []
    for p in range(3):
        axis = (p + 2) % 3
        base = (p * 3 + 2) * 4
        before, after = (coord[axis] + 3) % 4, (coord[axis] + 1) % 4
        hops[p][0].wait_recv()
        one = copy(view(p, 2, before, 0), g_sems, base + 2, ring[axis][1])
        hops[p][1].wait_recv()
        two = copy(view(p, 2, after, 8), g_sems, base + 3, ring[axis][3])
        forwards.append((one, two))
        last.append(copy(view(p, 2, before), g_sems, 37 + p * 4, pair))
        last.append(copy(view(p, 2, after), g_sems, 38 + p * 4, pair))
    for p in range(3):
        axis = (p + 2) % 3
        for made in forwards[p]:
            made.wait_recv()
        far = (coord[axis] + 2) % 4
        last.append(copy(view(p, 2, far), g_sems, 39 + p * 4, pair))
    for made in last:
        made.wait_recv()
    for made in started:
        made.wait_send()


def sum_spread(part, right):
    hbm = pl.BlockSpec(memory_space=pl.ANY)
    vmem = pl.BlockSpec(memory_space=pltpu.VMEM)
    return pl.pallas_call(
        sum_spread_kernel,
        out_shape=(
            jax.ShapeDtypeStruct((NS, 2, 4, 4, 4, 16, 256), f32),
            jax.ShapeDtypeStruct((16, 160, 128), f32),
        ),
        in_specs=[vmem, vmem],
        out_specs=(hbm, hbm),
        scratch_shapes=[
            pltpu.VMEM((NS, 8, 16, 256), f32),
            pltpu.VMEM((8, 160, 128), f32),
            pltpu.VMEM((7, NS, 16, 256), f32),
            pltpu.VMEM((7, 160, 128), f32),
            pltpu.VMEM((NS, 16, 256), f32),
            pltpu.VMEM((160, 128), f32),
            pltpu.SemaphoreType.DMA((16,)),
            pltpu.SemaphoreType.DMA((16,)),
            pltpu.SemaphoreType.DMA((48,)),
            pltpu.SemaphoreType.DMA((48,)),
            pltpu.SemaphoreType.DMA((8,)),
            pltpu.SemaphoreType.DMA((8,)),
            pltpu.SemaphoreType.DMA((2,)),
        ],
        compiler_params=pltpu.CompilerParams(
            collective_id=3, has_side_effects=True, vmem_limit_bytes=40 * 1024 * 1024
        ),
    )(part.reshape(NS, 2, 8, 16, 256), right.reshape(2, 8, 160, 128))

N = 2560
NB = N // B
RC = 128
CLASSES = ((0, 3, 9), (3, 6, 6), (6, 10, 3))


def cut(k, width=B):
    return slice(k * B, k * B + width)


def prod(left, right, dims):
    lh, ll = left
    rh, rl = right
    return mm(lh, rh, dims) + (mm(ll, rh, dims) + mm(lh, rl, dims))


def chain(left, right, dims):
    lh, ll = left
    rh, rl = right
    axis = dims[0][1][0]
    return mm(jnp.concatenate([lh, ll, lh], 1), jnp.concatenate([rh, rh, rl], axis), dims)


def factor_kernel(
    g_hbm, r_ref, o_ref, g, low, y_low, y, w_low, diag, panel, y_panel,
    second, rest, l21_low, a1_low, low1_low, live, sems,
):
    row = lax.broadcasted_iota(jnp.int32, (B, B), 0)
    col = lax.broadcasted_iota(jnp.int32, (B, B), 1)

    copies = [pltpu.make_async_copy(g_hbm.at[s], g.at[s], sems.at[s]) for s in range(NS)]
    for copy in copies:
        copy.start()

    live[0] = 1

    def lanes(k):
        return pl.ds(pl.multiple_of(k * B, B), B)

    def gram(i, k):
        b = jnp.minimum(10 * k - k * (k - 1) // 2 + i - k, 54)
        s, t = b // 8, b % 8
        tile = g[s, :, pl.ds((t // 4) * 2, 2), :, t % 4].reshape(B, B)
        return tile

    def gram_diag(k):
        tile = gram(k, k)
        return jnp.where(row == col, tile, SHRINK * tile)

    def rows_of(i, width):
        return low[i, :B, :width], low[i, B:, :width]

    def put(i, k, value):
        h, l = split(value)
        low[i, :B, lanes(k)] = h
        low[i, B:, lanes(k)] = l

    def put_y(k, value):
        y[:, lanes(k)] = value
        if isinstance(k, int) and k == NB - 1:
            return
        h, l = split(value)
        y_low[:RC, lanes(k)] = h
        y_low[RC:, lanes(k)] = l

    def w_of(k):
        return w_low[k, :B, :], w_low[k, B:, :]

    def step(k, width, tiles):
        if width == CLASSES[0][1] * B - B:

            @pl.when(k == 1)
            def _():
                for copy in copies[2:]:
                    copy.wait()

        old, now = (k + 1) % 2, k % 2
        last = jnp.maximum(k - 1, 0)
        targets = [jnp.minimum(k + 1 + r, NB) for r in range(tiles)]
        early = tiles // 3 + 1
        here = rows_of(k, width)

        def update(i):
            panel[now, i] = SHRINK * gram(i, k) - prod(rows_of(i, width), here, NT)

        @pl.when(live[0] == 1)
        def _():
            w1 = split(inverse_factor(diag[:H, :H]))
            w_old = w_of(last)
            for i in targets:
                put(i, last, prod(split(panel[old, i]), w_old, NT))
            put_y(last, prod(split(y_panel[old]), w_old, NT))
            for i in targets[:early]:
                update(i)
            for part in range(2):
                first = part * B
                w_low[k, first : first + H, :H] = w1[part]
                w_low[k, first : first + H, H:] = jnp.zeros((H, H), bf16)

        def w1_of():
            return w_low[k, :H, :H], w_low[k, B : B + H, :H]

        @pl.when(live[0] == 1)
        def _():
            l21 = chain(split(diag[H:, :H]), w1_of(), NT)
            l21s = split(l21)
            l21_low[...] = l21
            second[...] = diag[H:, H:] - chain(l21s, l21s, NT)

        @pl.when(live[0] == 1)
        def _():
            w2 = split(inverse_factor(second[...]))
            for i in targets[early:]:
                update(i)
            y_rows = y_low[:RC, :width], y_low[RC:, :width]
            y_panel[now] = r_ref[lanes(k), :].T - prod(y_rows, here, NT)
            mine = rows_of(k + 1, width)
            after = gram_diag(k + 1) - prod(mine, mine, NT)
            value = panel[now, k + 1]
            a1 = chain(split(value[:, :H]), w1_of(), NT)
            a1s = split(a1)
            a1_low[...] = a1
            diag[...] = after - chain(a1s, a1s, NT)
            rest[...] = value[:, H:] - chain(a1s, split(l21_low[...]), NT)
            low1_low[...] = chain(split(l21_low[...]), w1_of(), NN)
            for part in range(2):
                first = part * B + H
                w_low[k, first : first + H, H:] = w2[part]

        @pl.when(live[0] == 1)
        def _():
            w2s = w_low[k, H:B, H:], w_low[k, B + H :, H:]
            a2s = split(chain(split(rest[...]), w2s, NT))
            diag[...] = diag[...] - chain(a2s, a2s, NT)
            own = lanes(jnp.minimum(k, NB - 2))
            a1s = split(a1_low[...])
            low[k + 1, :B, own] = jnp.concatenate([a1s[0], a2s[0]], 1)
            low[k + 1, B:, own] = jnp.concatenate([a1s[1], a2s[1]], 1)
            w21 = split(-chain(w2s, split(low1_low[...]), NN))
            for part in range(2):
                first = part * B + H
                w_low[k, first : first + H, :H] = w21[part]

    for lo, hi, _ in CLASSES:
        zeros = jnp.zeros((2 * B, (hi - 1 - lo) * B), bf16)
        for i in range(lo, NB + 1):
            low[i, :, lo * B : (hi - 1) * B] = zeros
        y_low[:, lo * B : (hi - 1) * B] = jnp.zeros((2 * RC, (hi - 1 - lo) * B), bf16)
    panel[1] = jnp.zeros((NB + 1, B, B), f32)
    y_panel[1] = jnp.zeros((RC, B), f32)
    w_low[0] = jnp.zeros((2 * B, B), bf16)
    panel[0, NB] = jnp.zeros((B, B), f32)

    for copy in copies[:2]:
        copy.wait()
    diag[...] = gram_diag(0)
    for lo, hi, tiles in CLASSES:

        def one(k, _):
            step(k, (hi - 1) * B, tiles)
            return 0

        lax.fori_loop(lo, hi, one, 0)
    put_y(NB - 1, prod(split(y_panel[(NB - 1) % 2]), w_of(NB - 1), NT))
    for k in range(NB - 1, -1, -1):
        x = prod(split(y[:, cut(k)]), w_of(k), NN)
        o_ref[cut(k), :] = x.T.astype(bf16)
        xs = split(x)
        for j in range(k - 1, -1, -1):
            tile = low[k, :B, cut(j)], low[k, B:, cut(j)]
            y[:, cut(j)] = y[:, cut(j)] - prod(xs, tile, NN)


def factor_solve(gram, right):
    return pl.pallas_call(
        factor_kernel,
        out_shape=jax.ShapeDtypeStruct((N, RC), bf16),
        in_specs=[pl.BlockSpec(memory_space=pl.ANY), pl.BlockSpec(memory_space=pltpu.VMEM)],
        out_specs=pl.BlockSpec(memory_space=pltpu.VMEM),
        scratch_shapes=[
            pltpu.VMEM((NS, 2, 4, 4, 4, 16, 256), f32),
            pltpu.VMEM((NB + 1, 2 * B, N - B), bf16),
            pltpu.VMEM((2 * RC, N - B), bf16),
            pltpu.VMEM((RC, N), f32),
            pltpu.VMEM((NB, 2 * B, B), bf16),
            pltpu.VMEM((B, B), f32),
            pltpu.VMEM((2, NB + 1, B, B), f32),
            pltpu.VMEM((2, RC, B), f32),
            pltpu.VMEM((H, H), f32),
            pltpu.VMEM((B, H), f32),
            pltpu.VMEM((H, H), f32),
            pltpu.VMEM((B, H), f32),
            pltpu.VMEM((H, H), f32),
            pltpu.SMEM((1,), jnp.int32),
            pltpu.SemaphoreType.DMA((NS,)),
        ],
        compiler_params=pltpu.CompilerParams(vmem_limit_bytes=60 * 1024 * 1024),
    )(gram, right)


def local(acts, weights):
    at, wc = gather_acts(acts[0].T, weights[0])
    part, right = products(at.reshape(N, -1), wc.reshape(N, RC))
    gram, right = sum_spread(part, right)
    return factor_solve(gram, right.reshape(N, RC))


def solution(mesh):
    in_specs = (P("member", None, "tp"), P("member", "tp", None))
    return jax.shard_map(
        local, mesh=mesh, in_specs=in_specs, out_specs=P(None, "tp"), check_vma=False
    )
```

profile of v0, /device:TPU:1, one launch (start us, length us, event | category | flops | bytes accessed | tf_op | source)
XLA Modules:
  0.0 229.9 jit_solution(16198719099458076534)
XLA Ops:
  0.0 0.0 copy-start.1
  0.0 1.1 copy-done.1
  1.1 0.0 copy-start.2
  1.1 1.0 copy-done.2
  2.1 35.4 %shard_map.28 = (bf16[8,320,512]{2,1,0:T(8,128)(2,1)S(1)}, bf16[8,320,128]{2,1,0:T(8,128)(2,1)S(1)}) custom-call(bf16[320,512]{1,0:T(8,128)(2,1)S(1)} %bitcast.15, bf16[320,1024]{1,0:T(8,128)(2,1)S(1)} %bitcast.13), custom_call_target="tpu_custom_call" | custom-call | tf_op jit(solution)/shard_map/pallas_call | solution.py:189
  37.5 3.5 %shard_map.29 = (f32[7,256,256]{2,1,0:T(8,128)S(1)}, f32[2560,128]{1,0:T(8,128)S(1)}) custom-call(bf16[2560,512]{1,0:T(8,128)(2,1)S(1)} %bitcast.9, bf16[2560,128]{1,0:T(8,128)(2,1)S(1)} %bitcast.14), custom_call_target="tpu_custom_call" | custom-call | tf_op jit(solution)/shard_map/pallas_call | solution.py:232
  40.9 84.1 %shard_map.30 = (f32[7,2,4,4,4,16,256]{6,5,4,3,2,1,0:T(8,128)}, f32[16,160,128]{2,1,0:T(8,128)S(1)}) custom-call(f32[7,2,8,16,256]{4,3,2,1,0:T(8,128)S(1)} %bitcast.10, f32[2,8,160,128]{3,2,1,0:T(8,128)S(1)} %bitcast.12), custom_call_target="tpu_custom_call" | custom-call | tf_op jit(solution)/shard_map/pallas_call | solution.py:373
  125.0 0.0 copy-start
  125.0 1.1 copy-done
  126.1 103.6 %shard_map.31 = bf16[2560,128]{1,0:T(8,128)(2,1)} custom-call(f32[7,2,4,4,4,16,256]{6,5,4,3,2,1,0:T(8,128)} %get-tuple-element.15.g_hbm, f32[2560,128]{1,0:T(8,128)} %bitcast.11), custom_call_target="tpu_custom_call" | custom-call | tf_op jit(solution)/shard_map/pallas_call | solution.py:575
Async XLA Ops:
  0.0 1.1 copy-start.1
  1.1 1.0 copy-start.2
  125.0 1.1 copy-start
where the time goes:
time: 230 us
  Pallas kernels  227 us (99%)
  local copies, waits for them, and re-layouts  3.13 us (1%)
    pallas_call x1, Pallas kernels, factor_solve(): pl.pallas_call(factor_kernel, out_shape=jax.ShapeDtypeStruct((N, RC), bf1...  104 us
    pallas_call x1, Pallas kernels, sum_spread(): pl.pallas_call(sum_spread_kernel, out_shape=(jax.ShapeDtypeStruct((NS, 2,...  84.1 us
    pallas_call x1, Pallas kernels, gather_acts(): pl.pallas_call(gather_kernel, out_shape=(jax.ShapeDtypeStruct((8, width,...  35.4 us

commit v1 on v0

--- a/solution.py
+++ b/solution.py
@@ -98,7 +98,7 @@
 MESH = pl.DeviceIdType.MESH
 TN = (((0,), (0,)), ((), ()))
 NS = 7
-PARTS = ((0, 3), (3, 2), (5, 2))
+PARTS = ((0, 0, 2, None), (1, 2, 2, None), (2, 4, 2, None), (0, 6, 1, 0), (1, 6, 1, 8))
 
 
 def place():
@@ -295,17 +295,29 @@
     keep_g.start()
     keep_r.start()
 
-    def view(p, phase, value, rows=None):
-        order = (p, (p + 1) % 3, (p + 2) % 3)
+    def turn(n, phase):
+        return (PARTS[n][0] + phase) % 3
+
+    def view(n, phase, value, half=None):
+        axis, start, count, row = PARTS[n]
         index = list(coord)
-        for axis in order[:phase]:
-            index[axis] = pl.ds(0, 4)
-        index[order[phase]] = value
-        start, count = PARTS[p]
+        for earlier in range(phase):
+            index[(axis + earlier) % 3] = pl.ds(0, 4)
+        index[(axis + phase) % 3] = value
         index = [pl.ds(start, count), c] + index
-        if rows is not None:
-            index.append(pl.ds(rows, 8))
+        if row is not None:
+            index.append(pl.ds(row, 8))
+            if half is not None:
+                index.append(pl.ds(128 * half, 128))
+        elif half is not None:
+            index.append(pl.ds(8 * half, 8))
         return go_ref.at[tuple(index)]
+
+    def own_part(n):
+        _, start, count, row = PARTS[n]
+        if row is None:
+            return g_own.at[pl.ds(start, count)]
+        return g_own.at[pl.ds(start, count), pl.ds(row, 8)]
 
     def copy(ref, sems, i, peer, src=None):
         made = remote(ref if src is None else src, ref, sems[0].at[i], sems[1].at[i], peer)
@@ -314,53 +326,61 @@
         return made
 
     g_sems, r_sems = (gsend, grecv), (rsend, rrecv)
-    for phase in range(2):
-        waits = []
-        for p in range(3):
-            axis = (p + phase) % 3
-            mine = view(p, phase, coord[axis])
-            base = (p * 3 + phase) * 4
-            source = g_own.at[pl.ds(*PARTS[p])] if phase == 0 else None
-            for n, shift in enumerate((2, 1, 3)):
-                waits.append(copy(mine, g_sems, base + n, ring[axis][shift], source))
-        if phase == 0:
-            r_copies = [
-                copy(ro_ref.at[c * 8 + q], r_sems, d, peer, r_own)
-                for d, (_, peer) in enumerate(peers)
-            ]
-            keep_g.wait()
-            keep_r.wait()
-        for made in waits:
+    order = (2, 1, 4, 0, 3)
+
+    def spread_along(p, phase):
+        axis = turn(p, phase)
+        mine = view(p, phase, coord[axis])
+        base = p * 14 + phase * 3
+        source = own_part(p) if phase == 0 else None
+        return [
+            copy(mine, g_sems, base + n, ring[axis][shift], source)
+            for n, shift in enumerate((2, 1, 3))
+        ]
+
+    flying = {p: spread_along(p, 0) for p in range(5)}
+    keep_g.wait()
+    for p in order:
+        for made in flying[p]:
             made.wait_recv()
+        flying[p] = spread_along(p, 1)
+    r_copies = [
+        copy(ro_ref.at[c * 8 + q], r_sems, d, peer, r_own) for d, (_, peer) in enumerate(peers)
+    ]
     last = []
-    hops = []
-    for p in range(3):
-        axis = (p + 2) % 3
+    for p in order:
+        for made in flying[p]:
+            made.wait_recv()
+        axis = turn(p, 2)
         mine = view(p, 2, coord[axis])
-        base = (p * 3 + 2) * 4
-        hops.append((copy(mine, g_sems, base, ring[axis][1]), copy(mine, g_sems, base + 1, ring[axis][3])))
-        last.append(copy(mine, g_sems, 36 + p * 4, pair))
+        base = p * 14 + 6
+        flying[p] = (
+            copy(mine, g_sems, base, ring[axis][1]),
+            copy(mine, g_sems, base + 1, ring[axis][3]),
+        )
+        last.append(copy(mine, g_sems, p * 14 + 10, pair))
+    for p in order:
+        axis = turn(p, 2)
+        base = p * 14 + 6
+        before, after = (coord[axis] + 3) % 4, (coord[axis] + 1) % 4
+        one, two = flying[p]
+        one.wait_recv()
+        three = copy(view(p, 2, before, 0), g_sems, base + 2, ring[axis][1])
+        two.wait_recv()
+        four = copy(view(p, 2, after, 1), g_sems, base + 3, ring[axis][3])
+        flying[p] = (three, four)
+        last.append(copy(view(p, 2, before), g_sems, p * 14 + 11, pair))
+        last.append(copy(view(p, 2, after), g_sems, p * 14 + 12, pair))
+    keep_r.wait()
     for made in r_copies:
         made.wait_recv()
     last.append(copy(ro_ref.at[pl.ds(pl.multiple_of(c * 8, 8), 8)], r_sems, 7, pair))
-    forwards = []
-    for p in range(3):
-        axis = (p + 2) % 3
-        base = (p * 3 + 2) * 4
-        before, after = (coord[axis] + 3) % 4, (coord[axis] + 1) % 4
-        hops[p][0].wait_recv()
-        one = copy(view(p, 2, before, 0), g_sems, base + 2, ring[axis][1])
-        hops[p][1].wait_recv()
-        two = copy(view(p, 2, after, 8), g_sems, base + 3, ring[axis][3])
-        forwards.append((one, two))
-        last.append(copy(view(p, 2, before), g_sems, 37 + p * 4, pair))
-        last.append(copy(view(p, 2, after), g_sems, 38 + p * 4, pair))
-    for p in range(3):
-        axis = (p + 2) % 3
-        for made in forwards[p]:
+    for p in order:
+        axis = turn(p, 2)
+        for made in flying[p]:
             made.wait_recv()
         far = (coord[axis] + 2) % 4
-        last.append(copy(view(p, 2, far), g_sems, 39 + p * 4, pair))
+        last.append(copy(view(p, 2, far), g_sems, p * 14 + 13, pair))
     for made in last:
         made.wait_recv()
     for made in started:
@@ -387,8 +407,8 @@
             pltpu.VMEM((160, 128), f32),
             pltpu.SemaphoreType.DMA((16,)),
             pltpu.SemaphoreType.DMA((16,)),
-            pltpu.SemaphoreType.DMA((48,)),
-            pltpu.SemaphoreType.DMA((48,)),
+            pltpu.SemaphoreType.DMA((70,)),
+            pltpu.SemaphoreType.DMA((70,)),
             pltpu.SemaphoreType.DMA((8,)),
             pltpu.SemaphoreType.DMA((8,)),
             pltpu.SemaphoreType.DMA((2,)),

time: 230 us -> 222 us (0.965)
  Pallas kernels: 227 us -> 218 us
    pallas_call x1, Pallas kernels: 84.1 us -> 75.5 us  [sum_spread(): pl.pallas_call(sum_spread_kernel, out_shape=(jax.ShapeDtypeStruct((NS, 2,...]
where the time goes in v1:
time: 222 us; the launch traced here: 221 us
  Pallas kernels  218 us (98%)
  local copies, waits for them, and re-layouts  3.13 us (1%)
    pallas_call x1, Pallas kernels, factor_solve(): pl.pallas_call(factor_kernel, out_shape=jax.ShapeDtypeStruct((N, RC), bf1...  104 us
    pallas_call x1, Pallas kernels, sum_spread(): pl.pallas_call(sum_spread_kernel, out_shape=(jax.ShapeDtypeStruct((NS, 2,...  75.5 us
    pallas_call x1, Pallas kernels, gather_acts(): pl.pallas_call(gather_kernel, out_shape=(jax.ShapeDtypeStruct((8, width,...  35.4 us

profile of v1, /device:TPU:1, one launch (start us, length us, event | category | flops | bytes accessed | tf_op | source)
XLA Modules:
  0.0 221.3 jit_solution(9727447756663955677)
XLA Ops:
  0.0 0.0 copy-start.1
  0.0 1.1 copy-done.1
  1.1 0.0 copy-start.2
  1.1 1.0 copy-done.2
  2.1 35.4 %shard_map.28 = (bf16[8,320,512]{2,1,0:T(8,128)(2,1)S(1)}, bf16[8,320,128]{2,1,0:T(8,128)(2,1)S(1)}) custom-call(bf16[320,512]{1,0:T(8,128)(2,1)S(1)} %bitcast.15, bf16[320,1024]{1,0:T(8,128)(2,1)S(1)} %bitcast.13), custom_call_target="tpu_custom_call" | custom-call | tf_op jit(solution)/shard_map/pallas_call | solution.py:189
  37.5 3.5 %shard_map.29 = (f32[7,256,256]{2,1,0:T(8,128)S(1)}, f32[2560,128]{1,0:T(8,128)S(1)}) custom-call(bf16[2560,512]{1,0:T(8,128)(2,1)S(1)} %bitcast.9, bf16[2560,128]{1,0:T(8,128)(2,1)S(1)} %bitcast.14), custom_call_target="tpu_custom_call" | custom-call | tf_op jit(solution)/shard_map/pallas_call | solution.py:232
  40.9 75.5 %shard_map.30 = (f32[7,2,4,4,4,16,256]{6,5,4,3,2,1,0:T(8,128)}, f32[16,160,128]{2,1,0:T(8,128)S(1)}) custom-call(f32[7,2,8,16,256]{4,3,2,1,0:T(8,128)S(1)} %bitcast.10, f32[2,8,160,128]{3,2,1,0:T(8,128)S(1)} %bitcast.12), custom_call_target="tpu_custom_call" | custom-call | tf_op jit(solution)/shard_map/pallas_call | solution.py:393
  116.5 0.0 copy-start
  116.5 1.1 copy-done
  117.5 103.6 %shard_map.31 = bf16[2560,128]{1,0:T(8,128)(2,1)} custom-call(f32[7,2,4,4,4,16,256]{6,5,4,3,2,1,0:T(8,128)} %get-tuple-element.15.g_hbm, f32[2560,128]{1,0:T(8,128)} %bitcast.11), custom_call_target="tpu_custom_call" | custom-call | tf_op jit(solution)/shard_map/pallas_call | solution.py:595
Async XLA Ops:
  0.0 1.1 copy-start.1
  1.1 1.0 copy-start.2
  116.5 1.1 copy-start

commit v2 on v1

--- a/solution.py
+++ b/solution.py
@@ -269,31 +269,29 @@
     ]
     for copy in first:
         copy.start()
-    for copy in first:
-        copy.wait_recv()
-    g_pair[...] = g_pair[...] + g_ref[:, c]
-    r_pair[...] = r_pair[...] + r_ref[c]
-    second = []
+    second, third = [], []
     for d, (p, peer) in enumerate(peers):
         second.append(remote(g_pair.at[:, p], g_in.at[d], send.at[2 + d], recv.at[2 + d], peer))
-        second.append(remote(r_pair.at[p], r_in.at[d], send.at[9 + d], recv.at[9 + d], peer))
+        third.append(remote(r_pair.at[p], r_in.at[d], send.at[9 + d], recv.at[9 + d], peer))
+    first[0].wait_recv()
+    g_pair[...] = g_pair[...] + g_ref[:, c]
     for copy in second:
+        copy.start()
+    first[1].wait_recv()
+    r_pair[...] = r_pair[...] + r_ref[c]
+    for copy in third:
         copy.start()
     for copy in second:
         copy.wait_recv()
     g_sum = g_pair[:, q]
-    r_sum = r_pair[q]
     for d in range(7):
         g_sum = g_sum + g_in[d]
-        r_sum = r_sum + r_in[d]
     g_own[...] = g_sum
-    r_own[...] = r_sum
-    started = first + second
+    started = first + second + third
 
     keep_g = pltpu.make_async_copy(g_own, go_ref.at[:, c, x, y, z], own.at[0])
     keep_r = pltpu.make_async_copy(r_own, ro_ref.at[c * 8 + q], own.at[1])
     keep_g.start()
-    keep_r.start()
 
     def turn(n, phase):
         return (PARTS[n][0] + phase) % 3
@@ -344,6 +342,13 @@
         for made in flying[p]:
             made.wait_recv()
         flying[p] = spread_along(p, 1)
+    for made in third:
+        made.wait_recv()
+    r_sum = r_pair[q]
+    for d in range(7):
+        r_sum = r_sum + r_in[d]
+    r_own[...] = r_sum
+    keep_r.start()
     r_copies = [
         copy(ro_ref.at[c * 8 + q], r_sems, d, peer, r_own) for d, (_, peer) in enumerate(peers)
     ]

time: 222 us -> 216 us (0.973)
  Pallas kernels: 218 us -> 213 us
    pallas_call x1, Pallas kernels: 75.5 us -> 70.5 us  [sum_spread(): pl.pallas_call(sum_spread_kernel, out_shape=(jax.ShapeDtypeStruct((NS, 2,...]
where the time goes in v2:
time: 216 us
  Pallas kernels  213 us (99%)
  local copies, waits for them, and re-layouts  3.13 us (1%)
    pallas_call x1, Pallas kernels, factor_solve(): pl.pallas_call(factor_kernel, out_shape=jax.ShapeDtypeStruct((N, RC), bf1...  104 us
    pallas_call x1, Pallas kernels, sum_spread(): pl.pallas_call(sum_spread_kernel, out_shape=(jax.ShapeDtypeStruct((NS, 2,...  70.5 us
    pallas_call x1, Pallas kernels, gather_acts(): pl.pallas_call(gather_kernel, out_shape=(jax.ShapeDtypeStruct((8, width,...  35.4 us

profile of v2, /device:TPU:1, one launch (start us, length us, event | category | flops | bytes accessed | tf_op | source)
XLA Modules:
  0.0 216.3 jit_solution(5065104990272586504)
XLA Ops:
  0.0 0.0 copy-start.1
  0.0 1.1 copy-done.1
  1.1 0.0 copy-start.2
  1.1 1.0 copy-done.2
  2.1 35.4 %shard_map.28 = (bf16[8,320,512]{2,1,0:T(8,128)(2,1)S(1)}, bf16[8,320,128]{2,1,0:T(8,128)(2,1)S(1)}) custom-call(bf16[320,512]{1,0:T(8,128)(2,1)S(1)} %bitcast.15, bf16[320,1024]{1,0:T(8,128)(2,1)S(1)} %bitcast.13), custom_call_target="tpu_custom_call" | custom-call | tf_op jit(solution)/shard_map/pallas_call | solution.py:189
  37.5 3.5 %shard_map.29 = (f32[7,256,256]{2,1,0:T(8,128)S(1)}, f32[2560,128]{1,0:T(8,128)S(1)}) custom-call(bf16[2560,512]{1,0:T(8,128)(2,1)S(1)} %bitcast.9, bf16[2560,128]{1,0:T(8,128)(2,1)S(1)} %bitcast.14), custom_call_target="tpu_custom_call" | custom-call | tf_op jit(solution)/shard_map/pallas_call | solution.py:232
  40.9 70.5 %shard_map.30 = (f32[7,2,4,4,4,16,256]{6,5,4,3,2,1,0:T(8,128)}, f32[16,160,128]{2,1,0:T(8,128)S(1)}) custom-call(f32[7,2,8,16,256]{4,3,2,1,0:T(8,128)S(1)} %bitcast.10, f32[2,8,160,128]{3,2,1,0:T(8,128)S(1)} %bitcast.12), custom_call_target="tpu_custom_call" | custom-call | tf_op jit(solution)/shard_map/pallas_call | solution.py:398
  111.4 0.0 copy-start
  111.4 1.1 copy-done
  112.5 103.6 %shard_map.31 = bf16[2560,128]{1,0:T(8,128)(2,1)} custom-call(f32[7,2,4,4,4,16,256]{6,5,4,3,2,1,0:T(8,128)} %get-tuple-element.15.g_hbm, f32[2560,128]{1,0:T(8,128)} %bitcast.11), custom_call_target="tpu_custom_call" | custom-call | tf_op jit(solution)/shard_map/pallas_call | solution.py:600
Async XLA Ops:
  0.0 1.1 copy-start.1
  1.1 1.0 copy-start.2
  111.4 1.1 copy-start
